TPU v7x, 128 devices: a whole 4x4x4 slice. The times are simulated.
128 devices in a mesh: row: 8 (over x_lo, y), col: 16 (over x_hi, z, core).
Axes of the slice: x: 4 (x_hi: 2, x_lo: 2; x = x_hi * 2 + x_lo), y: 4, z: 4, core: 2. Of those that a mesh axis runs over, the one named last changes fastest.
Arguments:
- rhs: bfloat16 [1024, 2, 4096], P('col', None, 'row'), may hold values from -6 to 6
- solved: bfloat16 [1024, 49152], P(None, 'col'), may hold values from -6 to 6
- panel: bfloat16 [2, 4096, 49152], P(None, 'row', 'col'), may hold values from -0.02734375 to 0.02734375
- inverse: bfloat16 [2, 4096, 4096], P(None, 'row'), as said below
- link: bfloat16 [4096, 4096], P('row'), may hold values from -0.09375 to 0.09375
Outputs:
- solution: bfloat16 [1024, 2, 4096], P('col', None, 'row')
Inputs may be any that keep to these rules, and one draw needn't show every extreme that they name: Each inverse[b] is upper triangular with diagonal entries between 0.6 and 1.4.
All inputs are finite; a program needn't handle non-finite values.
Results may differ from a plain program's by a relative error of at most 0.0056.
Values may be sent and summed in bfloat16 or wider, within the bound.
A program may use at most 128 MiB of HBM per device.

v0:
```python
import jax
import jax.numpy as jnp
from jax import lax
from jax.sharding import PartitionSpec as P


def contract_rows(left, right):
    return lax.dot_general(
        left, right, (((1,), (1,)), ((), ())), preferred_element_type=jnp.float32
    )


def local(rhs, solved, panel, inverse, link):
    local_rows = panel.shape[1]
    flat_panel = panel.reshape(2 * local_rows, panel.shape[2])
    summed = lax.psum_scatter(
        contract_rows(solved, flat_panel), "col", scatter_dimension=0, tiled=True
    )
    first_sum = summed[:, :local_rows]
    second_sum = summed[:, local_rows:]
    first_res = (rhs[:, 0, :].astype(jnp.float32) - first_sum).astype(jnp.bfloat16)
    first_part = jnp.dot(first_res, inverse[0], preferred_element_type=jnp.float32)
    first_full = lax.psum(first_part, "row").astype(jnp.bfloat16)
    first_own = lax.dynamic_slice_in_dim(
        first_full, lax.axis_index("row") * local_rows, local_rows, 1
    )
    carried = contract_rows(first_full, link)
    second_res = (rhs[:, 1, :].astype(jnp.float32) - second_sum - carried).astype(jnp.bfloat16)
    second_part = jnp.dot(second_res, inverse[1], preferred_element_type=jnp.float32)
    second_own = lax.psum_scatter(second_part, "row", scatter_dimension=1, tiled=True).astype(
        jnp.bfloat16
    )
    return jnp.stack([first_own, second_own], axis=1)


def solution(mesh):
    return jax.shard_map(
        local,
        mesh=mesh,
        in_specs=(
            P("col", None, "row"),
            P(None, "col"),
            P(None, "row", "col"),
            P(None, "row", None),
            P("row", None),
        ),
        out_specs=P("col", None, "row"),
        check_vma=False,
    )
```

profile of v0, /device:TPU:0, one launch (start us, length us, event | category | flops | bytes accessed | tf_op | source)
XLA Modules:
  0.0 223.7 jit_solution(1169902966534646854)
XLA Ops:
  6.5 0.0 reduce-scatter.3.cloned.1.call-start
  6.5 0.0 copy-start
  6.5 12.0 %fusion.11 = f32[1024,1024]{1,0:T(8,128)} fusion(bf16[1024,3072]{1,0:T(8,128)(2,1)} %param.6, bf16[1024,3072]{1,0:T(8,128)(2,1)} %bitcast.27), kind=kOutput, calls=%fused_computation.18 | convolution fusion | flops 6442450944 | bytes 16777216 | tf_op jit(solution)/shard_map/dot_general | solution.py:8
  18.5 0.0 reduce-scatter.3.cloned.1.call-update
  18.6 0.0 reduce-scatter.5.cloned.1.call-start
  18.6 0.0 copy-done
  18.6 0.2 fusion.10
  18.8 83.1 %reduce-scatter.3.cloned.1.call-done = f32[64,1024]{1,0:T(8,128)} async-done(((f32[1024,1024]{1,0:T(8,128)}), f32[64,1024]{1,0:T(8,128)}) %reduce-scatter.3.cloned.1.call-update) | async-done | bytes 262160 | tf_op jit(solution)/shard_map/reduce_scatter | solution.py:16
  101.9 0.0 copy-start.1
  101.9 3.1 %fusion.2 = f32[64,4096]{1,0:T(8,128)S(1)} fusion(bf16[2,512,4096]{2,1,0:T(8,128)(2,1)} %param.8, f32[64,1024]{1,0:T(8,128)} %reduce-scatter.3.cloned.1.call-done, bf16[64,1,512]{2,1,0:T(2,128)(2,1)S(1)} %get-tuple-element.6), kind=kOutput, calls=%fused_computation.2 | convolution fusion | flops 268533760 | bytes 5439488 | tf_op jit(solution)/shard_map/dot_general | solution.py:22
  105.0 67.0 %all-reduce.1 = bf16[64,4096]{1,0:T(8,128)(2,1)S(1)} all-reduce(f32[64,4096]{1,0:T(8,128)S(1)} %fusion.2), channel_id=1, replica_groups=mesh['row'=8,'col'=16] {'row'}, use_global_device_ids=true, to_apply=%region_1.0 | all-reduce | flops 262144 | bytes 1572864 | tf_op jit(solution)/shard_map/psum | solution.py:23
  172.1 0.0 copy-done.1
  172.1 6.7 %fusion = f32[64,4096]{1,0:T(8,128)} fusion(bf16[2,512,4096]{2,1,0:T(8,128)(2,1)} %param.8, bf16[64,4096]{1,0:T(8,128)(2,1)S(1)} %all-reduce.1, bf16[512,4096]{1,0:T(8,128)(2,1)} %param.9, f32[64,1024]{1,0:T(8,128)S(1)} %copy-done.1, bf16[64,1,512]{2,1,0:T(2,128)(2,1)S(1)} %get-tuple-element.5), kind=kOutput, calls=%fused_computation | convolution fusion | flops 537001984 | bytes 10223616 | tf_op jit(solution)/shard_map/dot_general | solution.py:29
  178.7 0.0 reduce-scatter.5.cloned.1.call-update
  178.8 36.4 %reduce-scatter.5.cloned.1.call-done = f32[64,512]{1,0:T(8,128)} async-done(((f32[64,4096]{1,0:T(8,128)}), f32[64,512]{1,0:T(8,128)}) %reduce-scatter.5.cloned.1.call-update) | async-done | bytes 131088 | tf_op jit(solution)/shard_map/reduce_scatter | solution.py:30
  215.1 0.9 convert_bitcast_fusion
  216.1 0.8 copy.8
  (2 shorter events, 0.0 us)
Async XLA Ops:
  6.5 95.3 %reduce-scatter.3.cloned.1.call-start = ((), (), s32[]{:S(2)}) async-start(), calls=%async_computation.2 | async-start | bytes 4456448 | tf_op jit(solution)/shard_map/reduce_scatter | solution.py:16
  6.5 12.1 %copy-start = (bf16[64,2,512]{2,1,0:T(2,128)(2,1)S(1)}, bf16[64,2,512]{2,1,0:T(2,128)(2,1)}, u32[]{:S(2)}) copy-start(bf16[64,2,512]{2,1,0:T(2,128)(2,1)} %param.5) | copy-start | bytes 393220
  18.6 196.6 %reduce-scatter.5.cloned.1.call-start = ((), (), s32[]{:S(2)}) async-start(), calls=%async_computation.3 | async-start | bytes 1179648 | tf_op jit(solution)/shard_map/reduce_scatter | solution.py:30
  101.9 70.2 %copy-start.1 = (f32[64,1024]{1,0:T(8,128)S(1)}, f32[64,1024]{1,0:T(8,128)}, u32[]{:S(2)}) copy-start(f32[64,1024]{1,0:T(8,128)} %reduce-scatter.3.cloned.1.call-done) | copy-start | bytes 786436
Sparse Core Ops, SparseCore 0:
  18.7 83.1 reduce-scatter.2
  178.9 36.2 reduce-scatter.4
where the time goes:
time: 224 us
  waiting for transfers between devices  119 us (53%)
  blocking collectives  67 us (30%)
  matrix products  21.8 us (10%)
  between operations  13.5 us (6%)
    reduce_scatter x1, waiting for transfers between devices, local(): lax.psum_scatter(contract_rows(solved, flat_panel), 'col', scatter_dimens...  83.1 us
    psum x1, blocking collectives, local(): first_full = lax.psum(first_part, 'row').astype(jnp.bfloat16)  67 us
    reduce_scatter x1, waiting for transfers between devices, local(): lax.psum_scatter(second_part, 'row', scatter_dimension=1, tiled=True)  36.4 us
    dot_general x1, matrix products, contract_rows(): lax.dot_general(left, right, (((1,), (1,)), ((), ())), preferred_element_...  12 us
    dot_general x1, matrix products, local(): jnp.dot(second_res, inverse[1], preferred_element_type=jnp.float32)  6.65 us
  transfers between devices with their start and end apart: 2, of which 2 were waited for; matrix products, arithmetic and copies ran while one was open for 0% of the time, Pallas kernels for 0%

commit v1 on v0

--- a/solution.py
+++ b/solution.py
@@ -20,7 +20,7 @@
     second_sum = summed[:, local_rows:]
     first_res = (rhs[:, 0, :].astype(jnp.float32) - first_sum).astype(jnp.bfloat16)
     first_part = jnp.dot(first_res, inverse[0], preferred_element_type=jnp.float32)
-    first_full = lax.psum(first_part, "row").astype(jnp.bfloat16)
+    first_full = jnp.sum(lax.all_gather(first_part, "row"), axis=0).astype(jnp.bfloat16)
     first_own = lax.dynamic_slice_in_dim(
         first_full, lax.axis_index("row") * local_rows, local_rows, 1
     )

time: 224 us -> 254 us (1.13)
  waiting for transfers between devices: 119 us -> 212 us
  blocking collectives: 67 us -> 0 us
  other arithmetic: 0.93 us -> 4.91 us
    all_gather x0 -> x1, waiting for transfers between devices: none -> 90.8 us  [local(): lax.all_gather(first_part, 'row')]
    psum x1 -> x0, blocking collectives: 67 us -> none  [local(): first_full = lax.psum(first_part, 'row').astype(jnp.bfloat16)]
    reduce_sum x0 -> x1, other arithmetic: none -> 3.98 us  [local(): jnp.sum(lax.all_gather(first_part, 'row'), axis=0).astype(jnp.bfloat16)]
  transfers between devices with their start and end apart: 2 -> 3, of which waited for: 2 -> 3; matrix products, arithmetic and copies ran while one was open for 0% -> 0% of each run, Pallas kernels for 0% -> 0%
where the time goes in v1:
time: 254 us
  waiting for transfers between devices  212 us (83%)
  matrix products  22.8 us (9%)
  between operations  13.2 us (5%)
  other arithmetic  4.91 us (2%)
    all_gather x1, waiting for transfers between devices, local(): lax.all_gather(first_part, 'row')  90.8 us
    reduce_scatter x1, waiting for transfers between devices, local(): lax.psum_scatter(contract_rows(solved, flat_panel), 'col', scatter_dimens...  83.1 us
    reduce_scatter x1, waiting for transfers between devices, local(): lax.psum_scatter(second_part, 'row', scatter_dimension=1, tiled=True)  38 us
    dot_general x1, matrix products, contract_rows(): lax.dot_general(left, right, (((1,), (1,)), ((), ())), preferred_element_...  12 us
    dot_general x1, matrix products, local(): jnp.dot(second_res, inverse[1], preferred_element_type=jnp.float32)  6.63 us
  transfers between devices with their start and end apart: 3, of which 3 were waited for; matrix products, arithmetic and copies ran while one was open for 0% of the time, Pallas kernels for 0%

profile of v1, /device:TPU:0, one launch (start us, length us, event | category | flops | bytes accessed | tf_op | source)
XLA Modules:
  0.0 253.9 jit_solution(16175486301120991666)
XLA Ops:
  6.5 0.0 reduce-scatter.3.cloned.1.call-start
  6.5 0.0 copy-start
  6.5 12.0 %fusion.11 = f32[1024,1024]{1,0:T(8,128)} fusion(bf16[1024,3072]{1,0:T(8,128)(2,1)} %param.6, bf16[1024,3072]{1,0:T(8,128)(2,1)} %bitcast.29), kind=kOutput, calls=%fused_computation.18 | convolution fusion | flops 6442450944 | bytes 16777216 | tf_op jit(solution)/shard_map/dot_general | solution.py:8
  18.6 0.0 reduce-scatter.3.cloned.1.call-update
  18.6 0.0 all-gather.3.cloned.1.call-start
  18.6 0.0 copy-done
  18.6 0.2 fusion.10
  18.8 83.1 %reduce-scatter.3.cloned.1.call-done = f32[64,1024]{1,0:T(8,128)} async-done(((f32[1024,1024]{1,0:T(8,128)}), f32[64,1024]{1,0:T(8,128)}) %reduce-scatter.3.cloned.1.call-update) | async-done | bytes 262160 | tf_op jit(solution)/shard_map/reduce_scatter | solution.py:16
  101.9 4.2 %fusion.2 = f32[64,4096]{1,0:T(8,128)} fusion(bf16[2,512,4096]{2,1,0:T(8,128)(2,1)} %param.8, f32[64,1024]{1,0:T(8,128)} %reduce-scatter.3.cloned.1.call-done, bf16[64,1,512]{2,1,0:T(2,128)(2,1)S(1)} %get-tuple-element.6), kind=kOutput, calls=%fused_computation.2 | convolution fusion | flops 268533760 | bytes 5439488 | tf_op jit(solution)/shard_map/dot_general | solution.py:22
  106.1 0.0 copy-start.1
  106.1 0.0 all-gather.3.cloned.1.call-update
  106.1 0.0 reduce-scatter.5.cloned.1.call-start
  106.1 90.8 %all-gather.3.cloned.1.call-done = f32[512,4096]{1,0:T(8,128)} async-done(((f32[64,4096]{1,0:T(8,128)}), f32[512,4096]{1,0:T(8,128)}) %all-gather.3.cloned.1.call-update) | async-done | bytes 8388624 | tf_op jit(solution)/shard_map/all_gather | solution.py:23
  196.9 4.0 %reduce_sum.9 = bf16[64,4096]{1,0:T(8,128)(2,1)S(1)} reduce(f32[8,64,4096]{2,1,0:T(8,128)} %bitcast.28, f32[]{:T(128)} %constant.2.clone.1), dimensions={0}, to_apply=%region_1.0 | reduce | flops 1835008 | bytes 8912900 | tf_op jit(solution)/shard_map/reduce_sum | solution.py:23
  200.9 0.0 copy-done.1
  200.9 6.6 %fusion = f32[64,4096]{1,0:T(8,128)} fusion(bf16[2,512,4096]{2,1,0:T(8,128)(2,1)} %param.8, bf16[64,4096]{1,0:T(8,128)(2,1)S(1)} %reduce_sum.9, bf16[512,4096]{1,0:T(8,128)(2,1)} %param.9, f32[64,1024]{1,0:T(8,128)S(1)} %copy-done.1, bf16[64,1,512]{2,1,0:T(2,128)(2,1)S(1)} %get-tuple-element.5), kind=kOutput, calls=%fused_computation | convolution fusion | flops 537001984 | bytes 10223616 | tf_op jit(solution)/shard_map/dot_general | solution.py:29
  207.6 0.0 reduce-scatter.5.cloned.1.call-update
  207.6 38.0 %reduce-scatter.5.cloned.1.call-done = f32[64,512]{1,0:T(8,128)} async-done(((f32[64,4096]{1,0:T(8,128)}), f32[64,512]{1,0:T(8,128)}) %reduce-scatter.5.cloned.1.call-update) | async-done | bytes 131088 | tf_op jit(solution)/shard_map/reduce_scatter | solution.py:30
  245.6 0.9 convert_bitcast_fusion
  246.5 0.8 copy.8
  (2 shorter events, 0.0 us)
Async XLA Ops:
  6.5 95.4 %reduce-scatter.3.cloned.1.call-start = ((), (), s32[]{:S(2)}) async-start(), calls=%async_computation.2 | async-start | bytes 4456448 | tf_op jit(solution)/shard_map/reduce_scatter | solution.py:16
  6.5 12.1 %copy-start = (bf16[64,2,512]{2,1,0:T(2,128)(2,1)S(1)}, bf16[64,2,512]{2,1,0:T(2,128)(2,1)}, u32[]{:S(2)}) copy-start(bf16[64,2,512]{2,1,0:T(2,128)(2,1)} %param.5) | copy-start | bytes 393220
  18.6 178.4 %all-gather.3.cloned.1.call-start = ((), (), s32[]{:S(2)}) async-start(), calls=%async_computation.4 | async-start | bytes 9437184 | tf_op jit(solution)/shard_map/all_gather | solution.py:23
  106.1 94.9 %copy-start.1 = (f32[64,1024]{1,0:T(8,128)S(1)}, f32[64,1024]{1,0:T(8,128)}, u32[]{:S(2)}) copy-start(f32[64,1024]{1,0:T(8,128)} %reduce-scatter.3.cloned.1.call-done) | copy-start | bytes 786436
  106.1 139.5 %reduce-scatter.5.cloned.1.call-start = ((), (), s32[]{:S(2)}) async-start(), calls=%async_computation.3 | async-start | bytes 1179648 | tf_op jit(solution)/shard_map/reduce_scatter | solution.py:30
Sparse Core Ops, SparseCore 0:
  18.7 83.1 reduce-scatter.2
  106.2 90.6 all-gather.2
  207.7 37.8 reduce-scatter.4
